TPU v7x, 512 devices: a whole 4x8x8 slice. The times are simulated.
512 devices in a mesh: section: 8 (over y), replica: 64 (over z, x, core).
Axes of the slice: x: 4, y: 8, z: 8, core: 2. Of those that a mesh axis runs over, the one named last changes fastest.
Arguments:
- coords_in: bfloat16 [2, 8192, 512], P(None, 'replica'), may hold values from -6 to 6
- token_rows: bfloat16 [2, 8192, 2048], P(None, 'replica'), may hold values from -16 to 16
- cotangent: bfloat16 [2, 8192, 512], P(None, 'replica'), may hold values from -6 to 6
- subspace_basis: bfloat16 [512, 2048], replicated, may hold values from -0.25 to 0.25
- norm_gain: float32 [8, 2048], P('section'), may hold values from 0.5 to 1.5
- gate_weight: float32 [8, 2048, 256], P('section', 'replica'), may hold values from -0.125 to 0.125
- up_weight: bfloat16 [8, 2048, 256], P('section', 'replica'), may hold values from -0.125 to 0.125
- down_weight: float32 [8, 256, 512], P('section', 'replica'), may hold values from -0.375 to 0.375
- gate_moment: float32 [8, 2048, 256], P('section', 'replica'), may hold values from -0.625 to 0.625
- gate_second: float32 [8, 2048, 256], P('section', 'replica'), may hold values from 0.01 to 0.1
- down_moment: float32 [8, 256, 512], P('section', 'replica'), may hold values from -0.625 to 0.625
- down_second: float32 [8, 256, 512], P('section', 'replica'), may hold values from 0.01 to 0.1
Outputs:
- section_coords: bfloat16 [8, 2, 8192, 512], P('section', None, 'replica')
- coord_grads: bfloat16 [8, 2, 8192, 512], P('section', None, 'replica')
- gate_new: float32 [8, 2048, 256], P('section', 'replica')
- gate_moment_new: float32 [8, 2048, 256], P('section', 'replica')
- gate_second_new: float32 [8, 2048, 256], P('section', 'replica')
- down_new: float32 [8, 256, 512], P('section', 'replica')
- down_moment_new: float32 [8, 256, 512], P('section', 'replica')
- down_second_new: float32 [8, 256, 512], P('section', 'replica')
All inputs are finite; a program needn't handle non-finite values.
Results may differ from a plain program's by a relative error of at most 0.03.
Values may be sent and summed in bfloat16 or wider, within the bound.
A program may use at most 64 MiB of HBM per device.

v0:
```python
import math

import jax
import jax.numpy as jnp
from jax import lax
from jax.sharding import PartitionSpec as P

epsilon = 1e-06
learn_rate = 0.001
decay_first = 0.9
decay_second = 0.95
step_count = 10
adam_floor = 1e-08


def from_behind(value, axis, steps):
    count = lax.axis_size(axis)
    first, last = (max(0, -steps), min(count, count - steps))
    return lax.ppermute(value, axis, [(source, source + steps) for source in range(first, last)])


def contract_last(left, right):
    return lax.dot_general(
        left, right, (((1,), (1,)), ((), ())), preferred_element_type=jnp.float32
    )


def contract_first(left, right):
    return lax.dot_general(
        left, right, (((0,), (0,)), ((), ())), preferred_element_type=jnp.float32
    )


def silu_parts(gate_value):
    sigma = jax.nn.sigmoid(gate_value)
    return (gate_value * sigma, sigma * (1.0 + gate_value * (1.0 - sigma)))


def section_forward(coords, token_block, subspace_basis, gain_row, w_gate, w_up, w_down):
    expanded = jnp.dot(
        coords, subspace_basis, preferred_element_type=jnp.float32
    ) + token_block.astype(jnp.float32)
    inverse = lax.rsqrt(jnp.mean(expanded * expanded, axis=1, keepdims=True) + epsilon)
    normed = (expanded * inverse * gain_row).astype(jnp.bfloat16)
    gate_value = jnp.dot(normed, w_gate, preferred_element_type=jnp.float32)
    up_value = jnp.dot(normed, w_up, preferred_element_type=jnp.float32)
    active, slope_value = silu_parts(gate_value)
    hidden = (active * up_value).astype(jnp.bfloat16)
    output = (
        coords.astype(jnp.float32) + jnp.dot(hidden, w_down, preferred_element_type=jnp.float32)
    ).astype(jnp.bfloat16)
    return (output, (expanded, inverse, normed, gate_value, up_value, hidden))


def section_backward(next_grad, saved, subspace_basis, gain_row, w_gate, w_up, w_down):
    expanded, inverse, normed, gate_value, up_value, hidden = saved
    hidden_grad = contract_last(next_grad, w_down)
    down_term = contract_first(hidden, next_grad)
    active, slope_value = silu_parts(gate_value)
    gate_grad = (hidden_grad * up_value * slope_value).astype(jnp.bfloat16)
    up_grad = (hidden_grad * active).astype(jnp.bfloat16)
    gate_term = contract_first(normed, gate_grad)
    normed_grad = contract_last(gate_grad, w_gate) + contract_last(up_grad, w_up)
    scaled = normed_grad * gain_row
    centred = expanded * inverse
    expanded_grad = (
        inverse * (scaled - centred * jnp.mean(scaled * centred, axis=1, keepdims=True))
    ).astype(jnp.bfloat16)
    coord_grad = (
        next_grad.astype(jnp.float32) + contract_last(expanded_grad, subspace_basis)
    ).astype(jnp.bfloat16)
    return (coord_grad, gate_term, down_term)


def adam_update(weight_now, moment, second, gradient):
    moment_new = decay_first * moment + (1.0 - decay_first) * gradient
    second_new = decay_second * second + (1.0 - decay_second) * gradient * gradient
    update = (
        learn_rate
        * (moment_new / (1.0 - decay_first**step_count))
        / (jnp.sqrt(second_new / (1.0 - decay_second**step_count)) + adam_floor)
    )
    return (weight_now - update, moment_new, second_new)


def per_device(
    coords_in,
    token_rows,
    cotangent,
    subspace_basis,
    norm_gain,
    gate_weight,
    up_weight,
    down_weight,
    gate_moment,
    gate_second,
    down_moment,
    down_second,
):
    batches = coords_in.shape[0]
    rows_dev = coords_in.shape[1]
    coord_width = subspace_basis.shape[0]
    model_width = subspace_basis.shape[1]
    sections = lax.axis_size("section")
    section_index = lax.axis_index("section")
    tick_count = sections + batches - 1
    w_gate, w_up, w_down = (
        lax.all_gather(gate_weight[0].astype(jnp.bfloat16), "replica", axis=0, tiled=True),
        lax.all_gather(up_weight[0], "replica", axis=0, tiled=True),
        lax.all_gather(down_weight[0].astype(jnp.bfloat16), "replica", axis=0, tiled=True),
    )
    hidden_width = w_gate.shape[1]
    weights = (subspace_basis, norm_gain, w_gate, w_up, w_down)
    kept_buffers = (jnp.zeros((batches, rows_dev, coord_width), jnp.bfloat16),)
    produced = jnp.zeros((batches, rows_dev, coord_width), jnp.bfloat16)
    blank = jnp.zeros((rows_dev, coord_width), jnp.bfloat16)

    def forward_tick(carry, tick_now):
        incoming, produced, kept_buffers = carry
        batch_now = tick_now - section_index
        is_live = (batch_now >= 0) & (batch_now < batches)
        slot_index = jnp.clip(batch_now, 0, batches - 1)
        source = jnp.where(
            section_index == 0, lax.dynamic_index_in_dim(coords_in, slot_index, 0, False), incoming
        )
        token_block = lax.dynamic_index_in_dim(token_rows, slot_index, 0, False)

        def forward_run_layer(buffers):
            produced_now, kept_now = buffers
            output, saved = section_forward(source, token_block, *weights)
            produced_now = lax.dynamic_update_index_in_dim(produced_now, output, slot_index, 0)
            entries = (source,)
            kept_now = tuple(
                (
                    lax.dynamic_update_index_in_dim(buffer, item, slot_index, 0)
                    for buffer, item in zip(kept_now, entries)
                )
            )
            return (produced_now, kept_now)

        produced, kept_buffers = lax.cond(
            is_live, forward_run_layer, lambda unchanged: unchanged, (produced, kept_buffers)
        )
        outgoing = lax.dynamic_index_in_dim(produced, slot_index, 0, False)
        incoming = from_behind(outgoing, "section", 1)
        return ((incoming, produced, kept_buffers), None)

    (incoming, produced, kept_buffers), unused = lax.scan(
        forward_tick, (blank, produced, kept_buffers), jnp.arange(tick_count, dtype=jnp.int32)
    )

    def backward_tick(carry, tick_now):
        incoming, returned, gate_acc, down_acc = carry
        batch_now = tick_now - (sections - 1 - section_index)
        is_live = (batch_now >= 0) & (batch_now < batches)
        slot_index = jnp.clip(batch_now, 0, batches - 1)
        next_grad = jnp.where(
            section_index == sections - 1,
            lax.dynamic_index_in_dim(cotangent, slot_index, 0, False),
            incoming,
        )

        def backward_run_layer(buffers):
            returned_now, gate_now, down_now = buffers
            source = lax.dynamic_index_in_dim(kept_buffers[0], slot_index, 0, False)
            token_block = lax.dynamic_index_in_dim(token_rows, slot_index, 0, False)
            saved = section_forward(source, token_block, *weights)[1]
            coord_grad, gate_term, down_term = section_backward(next_grad, saved, *weights)
            returned_now = lax.dynamic_update_index_in_dim(returned_now, coord_grad, slot_index, 0)
            return (returned_now, gate_now + gate_term, down_now + down_term)

        returned, gate_acc, down_acc = lax.cond(
            is_live, backward_run_layer, lambda unchanged: unchanged, (returned, gate_acc, down_acc)
        )
        outgoing = lax.dynamic_index_in_dim(returned, slot_index, 0, False)
        incoming = from_behind(outgoing, "section", -1)
        return ((incoming, returned, gate_acc, down_acc), None)

    returned = jnp.zeros((batches, rows_dev, coord_width), jnp.bfloat16)
    gate_zero = jnp.zeros((model_width, hidden_width), jnp.float32)
    down_zero = jnp.zeros((hidden_width, coord_width), jnp.float32)
    (incoming, returned, gate_acc, down_acc), unused = lax.scan(
        backward_tick,
        (blank, returned, gate_zero, down_zero),
        jnp.arange(tick_count, dtype=jnp.int32),
    )
    gate_share, down_share = (
        lax.psum_scatter(gate_acc, "replica", scatter_dimension=0, tiled=True),
        lax.psum_scatter(down_acc, "replica", scatter_dimension=0, tiled=True),
    )
    grad_scale = 1.0 / math.sqrt(batches * rows_dev * lax.axis_size("replica"))
    gate_new, gate_moment_new, gate_second_new = adam_update(
        gate_weight[0], gate_moment[0], gate_second[0], gate_share * grad_scale
    )
    down_new, down_moment_new, down_second_new = adam_update(
        down_weight[0], down_moment[0], down_second[0], down_share * grad_scale
    )
    return (
        produced[None],
        returned[None],
        gate_new[None],
        gate_moment_new[None],
        gate_second_new[None],
        down_new[None],
        down_moment_new[None],
        down_second_new[None],
    )


def solution(mesh):
    placed = (
        P(None, "replica", None),
        P(None, "replica", None),
        P(None, "replica", None),
        P(),
        P("section", None),
        P("section", "replica", None),
        P("section", "replica", None),
        P("section", "replica", None),
        P("section", "replica", None),
        P("section", "replica", None),
        P("section", "replica", None),
        P("section", "replica", None),
    )
    return jax.shard_map(
        per_device,
        mesh=mesh,
        in_specs=placed,
        out_specs=(
            P("section", None, "replica", None),
            P("section", None, "replica", None),
            P("section", "replica", None),
            P("section", "replica", None),
            P("section", "replica", None),
            P("section", "replica", None),
            P("section", "replica", None),
            P("section", "replica", None),
        ),
        check_vma=False,
    )
```

profile of v0, /device:TPU:1, one launch (start us, length us, event | category | flops | bytes accessed | tf_op | source)
XLA Modules:
  0.0 802.1 jit_solution(16639715585179184832)
XLA Ops:
  10.1 51.6 %all-gather.1 = bf16[64,4,512]{2,1,0:T(4,128)(2,1)S(1)} all-gather(bf16[1,4,512]{2,1,0:T(4,128)(2,1)S(1)} %fusion.30), channel_id=1, replica_groups=mesh['section'=8,'replica'=64] {'replica'}, dimensions={0}, use_global_device_ids=true | all-gather | bytes 266240 | tf_op jit(solution)/shard_map/all_gather | solution.py:110
  61.8 38.6 %all-gather.5.cloned.1.call-done = bf16[2048,256]{1,0:T(8,128)(2,1)} async-done(((bf16[32,256]{1,0:T(8,128)(2,1)}), bf16[2048,256]{1,0:T(8,128)(2,1)}) %all-gather.5.cloned.1.call-update) | async-done | bytes 1048592 | tf_op jit(solution)/shard_map/all_gather | solution.py:108
  100.4 83.1 %all-gather.7.cloned.1.call-done = bf16[1,2048,256]{2,1,0:T(8,128)(2,1)} async-done(((bf16[1,32,256]{2,1,0:T(8,128)(2,1)}), bf16[1,2048,256]{2,1,0:T(8,128)(2,1)}) %all-gather.7.cloned.1.call-update) | async-done | bytes 1048592 | tf_op jit(solution)/shard_map/all_gather | solution.py:109
  184.2 97.7 %while.33 = (s32[]{:T(128)}, bf16[128,512]{1,0:T(8,128)(2,1)S(1)}, bf16[2,128,512]{2,1,0:T(8,128)(2,1)}, bf16[2,128,512]{2,1,0:T(8,128)(2,1)S(1)}, s32[9]{0:T(12...) while((s32[]{:T(128)}, bf16[128,512]{1,0:T(8,128)(2,1)S(1)}, ...), condition=%wide.region_4.5_spmd, body=%wide.region_0.4_spmd.sunk | while | flops 573505664 | bytes 18533412 | solution.py:148
  185.5 5.0 conditional.4
  186.6 2.3 multiply_reduce_fusion
  192.7 3.0 collective-permute-done
  196.9 5.0 conditional.4
  198.0 2.3 multiply_reduce_fusion
  202.9 4.1 collective-permute-start
  207.0 1.9 collective-permute-done
  211.1 9.3 %collective-permute-start = (bf16[128,512]{1,0:T(8,128)(2,1)S(1)}, bf16[128,512]{1,0:T(8,128)(2,1)S(1)}, u32[]{:S(2)}, u32[]{:S(2)}) collective-permute-start(bf16[128,512]{1,0:T(8,128)(2,1)S(1)} %dynamic-slice_bitcast_fusion.4), channel_id=1, source_target_pairs={{0,64},{64,128},{128,192},{192,256},{256,320},{320,384},{384,448},... | collective-permute-start | bytes 393224 | tf_op jit(solution)/shard_map/while/body/eval_jaxpr/ppermute | solution.py:19
  224.5 3.8 collective-permute-start
  232.4 7.2 collective-permute-start
  243.8 3.8 collective-permute-start
  251.7 6.9 collective-permute-start
  262.7 3.8 collective-permute-start
  270.6 9.4 %collective-permute-start = (bf16[128,512]{1,0:T(8,128)(2,1)S(1)}, bf16[128,512]{1,0:T(8,128)(2,1)S(1)}, u32[]{:S(2)}, u32[]{:S(2)}) collective-permute-start(bf16[128,512]{1,0:T(8,128)(2,1)S(1)} %dynamic-slice_bitcast_fusion.4), channel_id=1, source_target_pairs={{0,64},{64,128},{128,192},{192,256},{256,320},{320,384},{384,448},... | collective-permute-start | bytes 393224 | tf_op jit(solution)/shard_map/while/body/eval_jaxpr/ppermute | solution.py:19
  284.2 161.7 %while.34 = (s32[]{:T(128)}, bf16[128,512]{1,0:T(8,128)(2,1)S(1)}, bf16[2,128,512]{2,1,0:T(8,128)(2,1)}, f32[2048,256]{1,0:T(8,128)}, f32[256,512]{1,0:T(8,128)S...) while((s32[]{:T(128)}, bf16[128,512]{1,0:T(8,128)(2,1)S(1)}, ...), condition=%wide.region_10.11_spmd, body=%wide.region_5.10_spmd.sunk | while | flops 1281163392 | bytes 53303908 | solution.py:182
  287.7 6.0 collective-permute-done.1
  297.3 6.8 collective-permute-done.1
  307.5 6.6 collective-permute-done.1
  317.6 7.3 collective-permute-done.1
  328.4 7.6 collective-permute-done.1
  339.5 7.2 collective-permute-done.1
  350.2 61.5 %collective-permute-done.1 = bf16[128,512]{1,0:T(8,128)(2,1)S(1)} collective-permute-done((bf16[128,512]{1,0:T(8,128)(2,1)S(1)}, bf16[128,512]{1,0:T(8,128)(2,1)S(1)}, u32[]{:S(2)}, u32[]{:S(2)}) %collective-permute-start.1) | collective-permute-done | bytes 131104 | tf_op jit(solution)/shard_map/while/body/eval_jaxpr/ppermute | solution.py:19
  412.9 8.6 %conditional.5 = ((bf16[2,128,512]{2,1,0:T(8,128)(2,1)}, f32[2048,256]{1,0:T(8,128)}, f32[256,512]{1,0:T(8,128)S(1)})) conditional(s32[]{:T(128)} %convert_element_type.126, (bf16[2,128,512]{2,1,0:T(8,128)(2,1)}, f32[2048,256]{1,0:T(8,128)}, f32[256,512]{1,0:T(8,128)S(1)}) %tuple.84, (pred[]{:T(512)}, bf16[2,128,512]{2,1,0:T(8,128)(2,1)}, s32[]{:T(128)}, ...), branch_computations={%region_6.6_spmd, %region_7.9_spmd} | conditional | flops 1281163392 | bytes 52517052 | solution.py:172
  423.8 5.6 collective-permute-done.1
  430.6 8.6 %conditional.5 = ((bf16[2,128,512]{2,1,0:T(8,128)(2,1)}, f32[2048,256]{1,0:T(8,128)}, f32[256,512]{1,0:T(8,128)S(1)})) conditional(s32[]{:T(128)} %convert_element_type.126, (bf16[2,128,512]{2,1,0:T(8,128)(2,1)}, f32[2048,256]{1,0:T(8,128)}, f32[256,512]{1,0:T(8,128)S(1)}) %tuple.84, (pred[]{:T(512)}, bf16[2,128,512]{2,1,0:T(8,128)(2,1)}, s32[]{:T(128)}, ...), branch_computations={%region_6.6_spmd, %region_7.9_spmd} | conditional | flops 1281163392 | bytes 52517052 | solution.py:172
  441.5 4.4 collective-permute-done.1
  449.2 197.1 %all-reduce.3.cloned.1.call-done = f32[256,512]{1,0:T(8,128)} async-done(((f32[256,512]{1,0:T(8,128)}), f32[256,512]{1,0:T(8,128)}) %all-reduce.3.cloned.1.call-update) | async-done | bytes 524304
  647.7 146.4 %reduce-scatter.2.cloned.1.call-done = f32[32,256]{1,0:T(8,128)} async-done(((f32[2048,256]{1,0:T(8,128)}), f32[32,256]{1,0:T(8,128)}) %reduce-scatter.2.cloned.1.call-update) | async-done | bytes 32784 | tf_op jit(solution)/shard_map/reduce_scatter | solution.py:188
  (170 shorter events, 87.3 us)
Async XLA Ops:
  7.2 93.2 %all-gather.5.cloned.1.call-start = ((), (), s32[]{:S(2)}) async-start(), calls=%async_computation.1 | async-start | bytes 1064960 | tf_op jit(solution)/shard_map/all_gather | solution.py:108
  8.6 174.9 %all-gather.7.cloned.1.call-start = ((), (), s32[]{:S(2)}) async-start(), calls=%async_computation.3 | async-start | bytes 1064960 | tf_op jit(solution)/shard_map/all_gather | solution.py:109
  9.4 637.0 %all-reduce.3.cloned.1.call-start = ((), (), s32[]{:S(2)}) async-start(), calls=%async_computation.4 | async-start | bytes 1048576
  185.5 3.4 copy-start.3
  185.5 3.4 copy-start.8
  191.4 4.3 collective-permute-start
  197.0 3.4 copy-start.3
  197.0 3.4 copy-start.8
  202.9 6.0 collective-permute-start
  211.1 11.2 %collective-permute-start = (bf16[128,512]{1,0:T(8,128)(2,1)S(1)}, bf16[128,512]{1,0:T(8,128)(2,1)S(1)}, u32[]{:S(2)}, u32[]{:S(2)}) collective-permute-start(bf16[128,512]{1,0:T(8,128)(2,1)S(1)} %dynamic-slice_bitcast_fusion.4), channel_id=1, source_target_pairs={{0,64},{64,128},{128,192},{192,256},{256,320},{320,384},{384,448},... | collective-permute-start | bytes 393224 | tf_op jit(solution)/shard_map/while/body/eval_jaxpr/ppermute | solution.py:19
  224.5 5.7 collective-permute-start
  232.4 9.2 %collective-permute-start = (bf16[128,512]{1,0:T(8,128)(2,1)S(1)}, bf16[128,512]{1,0:T(8,128)(2,1)S(1)}, u32[]{:S(2)}, u32[]{:S(2)}) collective-permute-start(bf16[128,512]{1,0:T(8,128)(2,1)S(1)} %dynamic-slice_bitcast_fusion.4), channel_id=1, source_target_pairs={{0,64},{64,128},{128,192},{192,256},{256,320},{320,384},{384,448},... | collective-permute-start | bytes 393224 | tf_op jit(solution)/shard_map/while/body/eval_jaxpr/ppermute | solution.py:19
  243.8 5.7 collective-permute-start
  251.7 8.9 %collective-permute-start = (bf16[128,512]{1,0:T(8,128)(2,1)S(1)}, bf16[128,512]{1,0:T(8,128)(2,1)S(1)}, u32[]{:S(2)}, u32[]{:S(2)}) collective-permute-start(bf16[128,512]{1,0:T(8,128)(2,1)S(1)} %dynamic-slice_bitcast_fusion.4), channel_id=1, source_target_pairs={{0,64},{64,128},{128,192},{192,256},{256,320},{320,384},{384,448},... | collective-permute-start | bytes 393224 | tf_op jit(solution)/shard_map/while/body/eval_jaxpr/ppermute | solution.py:19
  262.7 5.7 collective-permute-start
  270.6 11.3 %collective-permute-start = (bf16[128,512]{1,0:T(8,128)(2,1)S(1)}, bf16[128,512]{1,0:T(8,128)(2,1)S(1)}, u32[]{:S(2)}, u32[]{:S(2)}) collective-permute-start(bf16[128,512]{1,0:T(8,128)(2,1)S(1)} %dynamic-slice_bitcast_fusion.4), channel_id=1, source_target_pairs={{0,64},{64,128},{128,192},{192,256},{256,320},{320,384},{384,448},... | collective-permute-start | bytes 393224 | tf_op jit(solution)/shard_map/while/body/eval_jaxpr/ppermute | solution.py:19
  286.4 7.3 collective-permute-start.1
  296.0 8.1 %collective-permute-start.1 = (bf16[128,512]{1,0:T(8,128)(2,1)S(1)}, bf16[128,512]{1,0:T(8,128)(2,1)S(1)}, u32[]{:S(2)}, u32[]{:S(2)}) collective-permute-start(bf16[128,512]{1,0:T(8,128)(2,1)S(1)} %dynamic-slice_bitcast_fusion.5), channel_id=1, source_target_pairs={{64,0},{128,64},{192,128},{256,192},{320,256},{384,320},{448,384},... | collective-permute-start | bytes 393224 | tf_op jit(solution)/shard_map/while/body/eval_jaxpr/ppermute | solution.py:19
  306.2 7.9 collective-permute-start.1
  316.3 8.6 %collective-permute-start.1 = (bf16[128,512]{1,0:T(8,128)(2,1)S(1)}, bf16[128,512]{1,0:T(8,128)(2,1)S(1)}, u32[]{:S(2)}, u32[]{:S(2)}) collective-permute-start(bf16[128,512]{1,0:T(8,128)(2,1)S(1)} %dynamic-slice_bitcast_fusion.5), channel_id=1, source_target_pairs={{64,0},{128,64},{192,128},{256,192},{320,256},{384,320},{448,384},... | collective-permute-start | bytes 393224 | tf_op jit(solution)/shard_map/while/body/eval_jaxpr/ppermute | solution.py:19
  327.0 8.9 %collective-permute-start.1 = (bf16[128,512]{1,0:T(8,128)(2,1)S(1)}, bf16[128,512]{1,0:T(8,128)(2,1)S(1)}, u32[]{:S(2)}, u32[]{:S(2)}) collective-permute-start(bf16[128,512]{1,0:T(8,128)(2,1)S(1)} %dynamic-slice_bitcast_fusion.5), channel_id=1, source_target_pairs={{64,0},{128,64},{192,128},{256,192},{320,256},{384,320},{448,384},... | collective-permute-start | bytes 393224 | tf_op jit(solution)/shard_map/while/body/eval_jaxpr/ppermute | solution.py:19
  338.2 8.5 %collective-permute-start.1 = (bf16[128,512]{1,0:T(8,128)(2,1)S(1)}, bf16[128,512]{1,0:T(8,128)(2,1)S(1)}, u32[]{:S(2)}, u32[]{:S(2)}) collective-permute-start(bf16[128,512]{1,0:T(8,128)(2,1)S(1)} %dynamic-slice_bitcast_fusion.5), channel_id=1, source_target_pairs={{64,0},{128,64},{192,128},{256,192},{320,256},{384,320},{448,384},... | collective-permute-start | bytes 393224 | tf_op jit(solution)/shard_map/while/body/eval_jaxpr/ppermute | solution.py:19
  348.9 62.8 %collective-permute-start.1 = (bf16[128,512]{1,0:T(8,128)(2,1)S(1)}, bf16[128,512]{1,0:T(8,128)(2,1)S(1)}, u32[]{:S(2)}, u32[]{:S(2)}) collective-permute-start(bf16[128,512]{1,0:T(8,128)(2,1)S(1)} %dynamic-slice_bitcast_fusion.5), channel_id=1, source_target_pairs={{64,0},{128,64},{192,128},{256,192},{320,256},{384,320},{448,384},... | collective-permute-start | bytes 393224 | tf_op jit(solution)/shard_map/while/body/eval_jaxpr/ppermute | solution.py:19
  422.5 6.9 collective-permute-start.1
  440.2 5.7 collective-permute-start.1
  445.9 200.5 %copy-start.13 = (f32[1,4,512]{2,1,0:T(4,128)S(1)}, f32[1,4,512]{2,1,0:T(4,128)}, u32[]{:S(2)}) copy-start(f32[1,4,512]{2,1,0:T(4,128)} %param.27) | copy-start | bytes 24580
  445.9 200.5 %copy-start.14 = (f32[1,4,512]{2,1,0:T(4,128)S(1)}, f32[1,4,512]{2,1,0:T(4,128)}, u32[]{:S(2)}) copy-start(f32[1,4,512]{2,1,0:T(4,128)} %param.31) | copy-start | bytes 24580
  445.9 200.5 %copy-start.15 = (f32[1,4,512]{2,1,0:T(4,128)S(1)}, f32[1,4,512]{2,1,0:T(4,128)}, u32[]{:S(2)}) copy-start(f32[1,4,512]{2,1,0:T(4,128)} %param.30) | copy-start | bytes 24580
  445.9 348.2 %copy-start.10 = (f32[1,32,256]{2,1,0:T(8,128)S(1)}, f32[1,32,256]{2,1,0:T(8,128)}, u32[]{:S(2)}) copy-start(f32[1,32,256]{2,1,0:T(8,128)} %param.25) | copy-start | bytes 98308
  445.9 348.2 %copy-start.11 = (f32[1,32,256]{2,1,0:T(8,128)S(1)}, f32[1,32,256]{2,1,0:T(8,128)}, u32[]{:S(2)}) copy-start(f32[1,32,256]{2,1,0:T(8,128)} %param.29) | copy-start | bytes 98308
  446.0 348.2 %copy-start.12 = (f32[1,32,256]{2,1,0:T(8,128)S(1)}, f32[1,32,256]{2,1,0:T(8,128)}, u32[]{:S(2)}) copy-start(f32[1,32,256]{2,1,0:T(8,128)} %param.28) | copy-start | bytes 98308
  446.7 347.4 %reduce-scatter.2.cloned.1.call-start = ((), (), s32[]{:S(2)}) async-start(), calls=%async_computation.2 | async-start | bytes 2129920 | tf_op jit(solution)/shard_map/reduce_scatter | solution.py:188
  (13 other events, 23.4 us)
Sparse Core Ops, SparseCore 0:
  11.9 88.3 all-gather.4
  103.7 79.7 all-gather.6
  446.9 199.4 all-reduce.2
  650.9 143.2 reduce-scatter.1
where the time goes:
time: 808 us; the launch traced here: 802 us
  waiting for transfers between devices  598 us (74%)
  starting transfers between devices  61.3 us (8%)
  blocking collectives  51.6 us (6%)
  local copies, waits for them, and re-layouts  35 us (4%)
  matrix products  19.5 us (2%)
  between operations  14.5 us (2%)
  loops' own time  13 us (2%)
  other arithmetic  9.4 us (1%)
    unnamed x5, waiting for transfers between devices  198 us
    reduce_scatter x1, waiting for transfers between devices, per_device(): lax.psum_scatter(gate_acc, 'replica', scatter_dimension=0, tiled=True)  146 us
    ppermute x18, waiting for transfers between devices, from_behind(): lax.ppermute(value, axis, [(source, source + steps) for source in range(f...  131 us
    all_gather x1, waiting for transfers between devices, per_device(): lax.all_gather(up_weight[0], 'replica', axis=0, tiled=True)  83.1 us
    ppermute x18, starting transfers between devices, from_behind(): lax.ppermute(value, axis, [(source, source + steps) for source in range(f...  61.2 us
    all_gather x1, blocking collectives, per_device(): lax.all_gather(down_weight[0].astype(jnp.bfloat16), 'replica', axis=0, ti...  51.6 us
    all_gather x1, waiting for transfers between devices, per_device(): lax.all_gather(gate_weight[0].astype(jnp.bfloat16), 'replica', axis=0, ti...  38.6 us
  transfers between devices with their start and end apart: 22, of which 22 were waited for; matrix products, arithmetic and copies ran while one was open for 0% of the time, Pallas kernels for 0%

commit v1 on v0

v1 whole, which is shorter than its diff:
```python
import math

import jax
import jax.numpy as jnp
from jax import lax
from jax.experimental import pallas as pl
from jax.experimental.pallas import tpu as pltpu
from jax.sharding import PartitionSpec as P

F32 = jnp.float32
BF16 = jnp.bfloat16
MESH = pl.DeviceIdType.MESH
epsilon = 1e-06
learn_rate = 0.001
decay_first = 0.9
decay_second = 0.95
step_count = 10
adam_floor = 1e-08

D, FF, K = 2048, 256, 512
ROWS = 256
PIECE = 32
PIECES = ROWS // PIECE
NZ, NX, NS = 8, 4, 8
CHUNK = D // NZ
GATHER_ROWS = 80
REDUCE_ROWS = 48
Z_ORDER = (1, 7, 2, 6, 3, 5, 4)


def dot_last(left, right):
    return lax.dot_general(left, right, (((1,), (1,)), ((), ())), preferred_element_type=F32)


def dot(left, right):
    return jnp.dot(left, right, preferred_element_type=F32)


def adam_update(weight_now, moment, second, gradient):
    moment_new = decay_first * moment + (1.0 - decay_first) * gradient
    second_new = decay_second * second + (1.0 - decay_second) * gradient * gradient
    update = (
        learn_rate
        * (moment_new / (1.0 - decay_first**step_count))
        / (jnp.sqrt(second_new / (1.0 - decay_second**step_count)) + adam_floor)
    )
    return (weight_now - update, moment_new, second_new)


def kernel(
    coords_hbm, tok_hbm, cot_hbm, basis_hbm, gain, gate_w, up_w, down_w, gate_m, gate_s, down_m, down_s,
    o_coords, o_grads, o_gw, o_gm, o_gs, o_dw, o_dm, o_ds,
    tok, basis, cin, gin, wbuf, lhs, acc_gp, acc_mt, mg, mt, wd, wdt, tok_sq, inv_s, gate_v, up_v, act_s, slope_s,
    e_s, hid, gg_s, norm_t, wide, narrow, stage, gsend, gcore, xsum, xrecv, zsum, zrecv,
    local_sem, az_s, az_r, ax_s, ax_r, ac_s, ac_r, f_s, f_r, b_s, b_r, rc_s, rc_r, rx_s, rx_r, rz_s, rz_r,
):
    s = lax.axis_index("section")
    r = lax.axis_index("replica")
    z = r // 8
    x = lax.rem(r // 2, 4)
    c = lax.rem(r, 2)

    def device(z_of, x_of, c_of):
        return (s, (z_of * 4 + x_of) * 2 + c_of)

    def z_at(k):
        return lax.rem(z + k + NZ, NZ)

    def x_at(k):
        return lax.rem(x + k + NX, NX)

    partner = device(z, x, 1 - c)

    def remote(source, target, send_sem, recv_sem, where):
        return pltpu.make_async_remote_copy(
            src_ref=source, dst_ref=target, send_sem=send_sem, recv_sem=recv_sem,
            device_id=where, device_id_type=MESH,
        )

    load_tok = pltpu.make_async_copy(tok_hbm, tok, local_sem.at[0])
    load_basis = pltpu.make_async_copy(basis_hbm, basis, local_sem.at[1])
    load_basis.start()
    load_tok.start()

    barrier = pltpu.get_barrier_semaphore()
    for k in range(1, NZ):
        pl.semaphore_signal(barrier, inc=1, device_id=device(z_at(k), x, c), device_id_type=MESH)
    for k in range(1, NX):
        pl.semaphore_signal(barrier, inc=1, device_id=device(z, x_at(k), c), device_id_type=MESH)
    pl.semaphore_signal(barrier, inc=1, device_id=partner, device_id_type=MESH)
    for k in (1, NS - 1):
        pl.semaphore_signal(barrier, inc=1, device_id=(lax.rem(s + k, NS), r), device_id_type=MESH)

    stage[...] = jnp.zeros_like(stage)
    for p in range(2):
        stage[4 * p : 4 * p + 4, :] = down_w[:, 256 * p : 256 * p + 256]
    wbuf[z, x, c, 0:32, :] = gate_w[...].astype(BF16)
    wbuf[z, x, c, 32:64, :] = up_w[...]
    wbuf[z, x, c, 64:80, :] = stage[...].astype(BF16)

    pl.semaphore_wait(barrier, NZ - 1 + NX - 1 + 1 + 2)

    def gather_z(k):
        return remote(wbuf.at[z, x, c], wbuf.at[z, x, c], az_s.at[k - 1], az_r.at[k - 1], device(z_at(k), x, c))

    def gather_x(j, k):
        block = wbuf.at[z_at(-j), x, c]
        return remote(block, block, ax_s.at[j, k - 1], ax_r.at[j, k - 1], device(z, x_at(k), c))

    def gather_c(j):
        block = wbuf.at[z_at(-j), pl.ds(0, NX), c]
        return remote(block, block, ac_s.at[j], ac_r.at[j], partner)

    for k in Z_ORDER:
        gather_z(k).start()
    for k in range(1, NX):
        gather_x(0, k).start()

    load_basis.wait()
    load_tok.wait()
    acc_gp[...] = jnp.zeros_like(acc_gp)
    square = jnp.zeros((ROWS, 1), F32)
    for j in range(NZ):
        cols = slice(CHUNK * j, CHUNK * (j + 1))
        b_now = basis[:, cols]
        t_now = tok[:, cols]
        acc_gp[0:K, :] += dot_last(b_now, b_now)
        acc_gp[K:, :] += dot_last(t_now, b_now)
        t32 = t_now.astype(F32)
        square = square + jnp.sum(t32 * t32, axis=1, keepdims=True)
        lhs[j, 0:K, :] = (b_now.astype(F32) * gain[:, cols]).astype(BF16)
        lhs[j, K:, :] = (t32 * gain[:, cols]).astype(BF16)
    tok_sq[...] = jnp.broadcast_to(square, tok_sq.shape)
    mg[:, K:] = acc_gp[0:K, :].astype(BF16)
    acc_mt[...] = jnp.zeros_like(acc_mt)

    for k in Z_ORDER:
        gather_z(k).wait_recv()
        for m in range(1, NX):
            gather_x(k, m).start()
    for j in (0,) + Z_ORDER:
        for m in range(1, NX):
            gather_x(j, m).wait_recv()
        gather_c(j).start()
    for j in (0,) + Z_ORDER:
        gather_c(j).wait_recv()
        at = z_at(-j)
        left = lhs[at]
        acc_mt[:, 0:FF] += dot(left, wbuf[at, :, :, 0:32, :].reshape(CHUNK, FF))
        acc_mt[:, FF:] += dot(left, wbuf[at, :, :, 32:64, :].reshape(CHUNK, FF))
    mg[:, 0:K] = acc_mt[0:K, :].astype(BF16)
    for h in range(2):
        wide[h] = wbuf[:, :, :, 64:80, 128 * h : 128 * h + 128].astype(F32).reshape(1024, 128)
    for p in range(2):
        for h in range(2):
            for i in range(4):
                narrow[2 * p + h, pl.ds(i, 64, stride=4), :] = wide[h, pl.ds(4 * p + i, 64, stride=16), :]
    for q in range(4):
        wd[:, 128 * q : 128 * q + 128] = narrow[q].astype(BF16)

    @pl.when(s == 0)
    def _():
        copy = pltpu.make_async_copy(coords_hbm, cin, local_sem.at[2])
        copy.start()
        copy.wait()

    @pl.when(s == NS - 1)
    def _():
        copy = pltpu.make_async_copy(cot_hbm, gin, local_sem.at[3])
        copy.start()
        copy.wait()

    def rows_of(i):
        return pl.ds(pl.multiple_of(i * PIECE, PIECE), PIECE)

    def relay_forward(i):
        return remote(o_coords.at[rows_of(i)], cin.at[rows_of(i)], f_s.at[i], f_r.at[i], (lax.rem(s + 1, NS), r))

    def relay_backward(i):
        return remote(o_grads.at[rows_of(i)], gin.at[rows_of(i)], b_s.at[i], b_r.at[i], (lax.rem(s + NS - 1, NS), r))

    def forward(i):
        rows = rows_of(i)

        @pl.when(s > 0)
        def _():
            relay_forward(i).wait_recv()

        now = cin[rows, :]
        now32 = now.astype(F32)
        product = dot(now, mg[...])
        side = acc_gp[pl.ds(pl.multiple_of(K + i * PIECE, PIECE), PIECE), :]
        e_now = product[:, K:] + side
        total = jnp.sum(now32 * (e_now + side), axis=1, keepdims=True) + tok_sq[rows, 0:1]
        inverse = lax.rsqrt(jnp.maximum(total, 0.0) * (1.0 / D) + epsilon)
        both = inverse * (product[:, 0:K] + acc_mt[pl.ds(pl.multiple_of(K + i * PIECE, PIECE), PIECE), :])
        gate_value = both[:, 0:FF]
        up_value = both[:, FF:]
        sigma = jax.nn.sigmoid(gate_value)
        active = gate_value * sigma
        hidden = (active * up_value).astype(BF16)
        o_coords[rows, :] = (now32 + dot(hidden, wd[...])).astype(BF16)

        @pl.when(s < NS - 1)
        def _():
            relay_forward(i).start()

        hid[rows, :] = hidden
        inv_s[rows, :] = jnp.broadcast_to(inverse, (PIECE, 128))
        gate_v[rows, :] = gate_value
        up_v[rows, :] = up_value
        act_s[rows, :] = active
        slope_s[rows, :] = up_value * (sigma * (1.0 + gate_value * (1.0 - sigma)))
        e_s[rows, :] = e_now

    def backward(i):
        rows = rows_of(i)

        @pl.when(s < NS - 1)
        def _():
            relay_backward(i).wait_recv()

        now = gin[rows, :]
        hidden_grad = dot(now, wdt[...])
        gate_grad = (hidden_grad * slope_s[rows, :]).astype(BF16)
        up_grad = (hidden_grad * act_s[rows, :]).astype(BF16)
        inverse = inv_s[rows, 0:1]
        back = dot(gate_grad, mt[0:FF, :]) + dot(up_grad, mt[FF:, :])
        shared = jnp.sum(
            gate_grad.astype(F32) * gate_v[rows, :] + up_grad.astype(F32) * up_v[rows, :], axis=1, keepdims=True
        ) * (1.0 / D)
        o_grads[rows, :] = (now.astype(F32) + inverse * (back - (shared * inverse) * e_s[rows, :])).astype(BF16)

        @pl.when(s > 0)
        def _():
            relay_backward(i).start()

        gg_s[rows, :] = gate_grad

    def transposed():
        mt[...] = acc_mt[0:K, :].T.astype(BF16)
        wdt[...] = wd[...].astype(F32).T.astype(BF16)

    def normed():
        for j in range(NZ):
            cols = slice(CHUNK * j, CHUNK * (j + 1))
            value = dot(cin[...], basis[:, cols]) + tok[:, cols].astype(F32)
            value = value * inv_s[:, 0:1] * gain[:, cols]
            norm_t[j] = value.T.astype(BF16)

    first, last = s == 0, s == NS - 1

    def step(k, carry):
        is_prep = jnp.where(first, k == PIECES, k == 0)
        is_norm = jnp.where(last, k == 2 * PIECES + 1, k == PIECES + 1)
        is_f = jnp.where(
            first, k < PIECES,
            jnp.where(last, (lax.rem(k, 2) == 1) & (k < 2 * PIECES + 1), (k >= 1) & (k <= PIECES)),
        )
        f_at = jnp.where(first, k, jnp.where(last, (k - 1) // 2, k - 1))
        is_b = jnp.where(last, (lax.rem(k, 2) == 0) & (k >= 2), k >= PIECES + 2)
        b_at = jnp.where(last, (k - 2) // 2, k - PIECES - 2)

        @pl.when(is_prep)
        def _():
            transposed()

        @pl.when(is_f)
        def _():
            forward(f_at)

        @pl.when(is_norm)
        def _():
            normed()

        @pl.when(is_b)
        def _():
            backward(b_at)

        return carry

    lax.fori_loop(0, 2 * PIECES + 2, step, 0)

    down_sum = dot(hid[...].astype(F32).T.astype(BF16), gin[...])
    for q in range(4):
        narrow[q] = down_sum[:, 128 * q : 128 * q + 128]
    wide[...] = jnp.zeros_like(wide)
    for p in range(2):
        for h in range(2):
            for i in range(4):
                wide[h, pl.ds(4 * p + i, 64, stride=16), :] = narrow[2 * p + h, pl.ds(i, 64, stride=4), :]
    for h in range(2):
        gsend[:, :, :, 32:48, 128 * h : 128 * h + 128] = wide[h].reshape(NZ, NX, 2, 16, 128).astype(BF16)

    def reduce_c(j):
        at = z_at(j)
        return remote(gsend.at[at, pl.ds(0, NX), 1 - c], gcore.at[at], rc_s.at[j], rc_r.at[j], partner)

    def reduce_x(j, k):
        at = z_at(j)
        return remote(xsum.at[at, x_at(k)], xrecv.at[at, k - 1], rx_s.at[j, k - 1], rx_r.at[j, k - 1], device(z, x_at(k), c))

    def reduce_z(j):
        at = z_at(j)
        return remote(zsum.at[at], zrecv.at[j - 1], rz_s.at[j - 1], rz_r.at[j - 1], device(at, x, c))

    far_first = Z_ORDER[::-1] + (0,)
    for j in far_first:
        at = z_at(j)
        part = dot(norm_t[at], gg_s[...])
        gsend[at, :, :, 0:32, :] = part.reshape(NX, 2, 32, FF).astype(BF16)
        reduce_c(j).start()
    for j in far_first:
        at = z_at(j)
        reduce_c(j).wait_recv()
        xsum[at] = (gsend[at, :, c].astype(F32) + gcore[at].astype(F32)).astype(BF16)
        for k in range(1, NX):
            reduce_x(j, k).start()
    for j in far_first:
        at = z_at(j)
        total = xsum[at, x].astype(F32)
        for k in range(1, NX):
            reduce_x(j, k).wait_recv()
            total = total + xrecv[at, k - 1].astype(F32)
        if j == 0:
            own = total
        else:
            zsum[at] = total.astype(BF16)
            reduce_z(j).start()
    for j in Z_ORDER:
        reduce_z(j).wait_recv()
        own = own + zrecv[j - 1].astype(F32)

    own = own * (1.0 / math.sqrt(ROWS * 64))
    o_gw[...], o_gm[...], o_gs[...] = adam_update(gate_w[...], gate_m[...], gate_s[...], own[0:32, :])
    stage[...] = own[32:48, :]
    for p in range(2):
        half = slice(256 * p, 256 * p + 256)
        o_dw[:, half], o_dm[:, half], o_ds[:, half] = adam_update(
            down_w[:, half], down_m[:, half], down_s[:, half], stage[4 * p : 4 * p + 4, :]
        )

    for k in range(1, NZ):
        gather_z(k).wait_send()
        reduce_z(k).wait_send()
    for j in range(NZ):
        gather_c(j).wait_send()
        reduce_c(j).wait_send()
        for k in range(1, NX):
            gather_x(j, k).wait_send()
            reduce_x(j, k).wait_send()

    def left(i, carry):
        @pl.when(s < NS - 1)
        def _():
            relay_forward(i).wait_send()

        @pl.when(s > 0)
        def _():
            relay_backward(i).wait_send()

        return carry

    lax.fori_loop(0, PIECES, left, 0)


def per_device(
    coords_in, token_rows, cotangent, subspace_basis, norm_gain, gate_weight, up_weight, down_weight,
    gate_moment, gate_second, down_moment, down_second,
):
    dma = pltpu.SemaphoreType.DMA
    vmem = pltpu.VMEM
    whole = pl.BlockSpec(memory_space=pltpu.VMEM)
    left = pl.BlockSpec(memory_space=pl.ANY)
    outs = pl.pallas_call(
        kernel,
        name="training_step",
        out_shape=(
            jax.ShapeDtypeStruct((ROWS, K), BF16),
            jax.ShapeDtypeStruct((ROWS, K), BF16),
            jax.ShapeDtypeStruct((32, FF), F32),
            jax.ShapeDtypeStruct((32, FF), F32),
            jax.ShapeDtypeStruct((32, FF), F32),
            jax.ShapeDtypeStruct((4, K), F32),
            jax.ShapeDtypeStruct((4, K), F32),
            jax.ShapeDtypeStruct((4, K), F32),
        ),
        in_specs=[left, left, left, left] + [whole] * 8,
        out_specs=(whole,) * 8,
        scratch_shapes=[
            vmem((ROWS, D), BF16),
            vmem((K, D), BF16),
            vmem((ROWS, K), BF16),
            vmem((ROWS, K), BF16),
            vmem((NZ, NX, 2, GATHER_ROWS, FF), BF16),
            vmem((NZ, K + ROWS, CHUNK), BF16),
            vmem((K + ROWS, K), F32),
            vmem((K + ROWS, K), F32),
            vmem((K, 2 * K), BF16),
            vmem((K, K), BF16),
            vmem((FF, K), BF16),
            vmem((K, FF), BF16),
            vmem((ROWS, 128), F32),
            vmem((ROWS, 128), F32),
            vmem((ROWS, FF), F32),
            vmem((ROWS, FF), F32),
            vmem((ROWS, FF), F32),
            vmem((ROWS, FF), F32),
            vmem((ROWS, K), F32),
            vmem((ROWS, FF), BF16),
            vmem((ROWS, FF), BF16),
            vmem((NZ, CHUNK, ROWS), BF16),
            vmem((2, 1024, 128), F32),
            vmem((4, FF, 128), F32),
            vmem((16, FF), F32),
            vmem((NZ, NX, 2, REDUCE_ROWS, FF), BF16),
            vmem((NZ, NX, REDUCE_ROWS, FF), BF16),
            vmem((NZ, NX, REDUCE_ROWS, FF), BF16),
            vmem((NZ, NX - 1, REDUCE_ROWS, FF), BF16),
            vmem((NZ, REDUCE_ROWS, FF), BF16),
            vmem((NZ - 1, REDUCE_ROWS, FF), BF16),
            dma((4,)),
            dma((NZ - 1,)), dma((NZ - 1,)),
            dma((NZ, NX - 1)), dma((NZ, NX - 1)),
            dma((NZ,)), dma((NZ,)),
            dma((PIECES,)), dma((PIECES,)),
            dma((PIECES,)), dma((PIECES,)),
            dma((NZ,)), dma((NZ,)),
            dma((NZ, NX - 1)), dma((NZ, NX - 1)),
            dma((NZ - 1,)), dma((NZ - 1,)),
        ],
        compiler_params=pltpu.CompilerParams(
            collective_id=0, has_side_effects=True, vmem_limit_bytes=48 * 1024 * 1024
        ),
        cost_estimate=pl.CostEstimate(flops=4 * 10**9, bytes_accessed=6 * 10**6, transcendentals=10**5),
    )(
        coords_in.reshape(ROWS, K), token_rows.reshape(ROWS, D), cotangent.reshape(ROWS, K), subspace_basis, norm_gain,
        gate_weight[0], up_weight[0], down_weight[0], gate_moment[0], gate_second[0], down_moment[0], down_second[0],
    )
    return (outs[0].reshape(1, 2, ROWS // 2, K), outs[1].reshape(1, 2, ROWS // 2, K)) + tuple(o[None] for o in outs[2:])


def solution(mesh):
    by_rows = P(None, "replica", None)
    by_weight = P("section", "replica", None)
    placed = (by_rows, by_rows, by_rows, P(), P("section", None)) + (by_weight,) * 7
    coords = P("section", None, "replica", None)
    return jax.shard_map(
        per_device, mesh=mesh, in_specs=placed, out_specs=(coords, coords) + (by_weight,) * 6, check_vma=False
    )
```

time: 808 us -> 125 us (0.15)
  waiting for transfers between devices: 598 us -> 0 us
  Pallas kernels: 0 us -> 108 us
  starting transfers between devices: 61.3 us -> 0 us
  blocking collectives: 51.6 us -> 0 us
  matrix products: 19.5 us -> 0 us
  local copies, waits for them, and re-layouts: 35 us -> 15.5 us
  between operations: 14.5 us -> 0.67 us
  loops' own time: 13 us -> 0 us
  other arithmetic: 9.4 us -> 0 us
    unnamed x5 -> x0, waiting for transfers between devices: 198 us -> none
    reduce_scatter x1 -> x0, waiting for transfers between devices: 146 us -> none  [per_device(): lax.psum_scatter(gate_acc, 'replica', scatter_dimension=0, tiled=True)]
    ppermute x18 -> x0, waiting for transfers between devices: 131 us -> none  [from_behind(): lax.ppermute(value, axis, [(source, source + steps) for source in range(f...]
    all_gather x2 -> x0, waiting for transfers between devices: 122 us -> none  [the longest x1 83.1 us: per_device(): lax.all_gather(up_weight[0], 'replica', axis=0, tiled=True)]
    pallas_call x0 -> x1, Pallas kernels: none -> 108 us  [per_device(): pl.pallas_call(kernel, name='training_step', out_shape=(jax.ShapeDtypeStr...]
    ppermute x18 -> x0, starting transfers between devices: 61.2 us -> none  [from_behind(): lax.ppermute(value, axis, [(source, source + steps) for source in range(f...]
    all_gather x1 -> x0, blocking collectives: 51.6 us -> none  [per_device(): lax.all_gather(down_weight[0].astype(jnp.bfloat16), 'replica', axis=0, ti...]
    dot_general x24 -> x0, matrix products: 19.5 us -> none  [the longest x4 7.83 us: section_forward(): jnp.dot(coords, subspace_basis, preferred_element_type=jnp.float32)]
  transfers between devices with their start and end apart: 22 -> 0, of which waited for: 22 -> 0; matrix products, arithmetic and copies ran while one was open for 0% -> 0% of each run, Pallas kernels for 0% -> 0%
where the time goes in v1:
time: 125 us; the launch traced here: 124 us
  Pallas kernels  108 us (86%)
  local copies, waits for them, and re-layouts  15.5 us (12%)
    pallas_call x1, Pallas kernels, per_device(): pl.pallas_call(kernel, name='training_step', out_shape=(jax.ShapeDtypeStr...  108 us
    unnamed x32, local copies, waits for them, and re-layouts  15.5 us

profile of v1, /device:TPU:1, one launch (start us, length us, event | category | flops | bytes accessed | tf_op | source)
XLA Modules:
  0.0 124.5 jit_solution(13240795630753912306)
XLA Ops:
  0.6 0.0 copy-start
  0.6 1.6 %copy-done = bf16[512,2048]{1,0:T(8,128)(2,1)S(1)} copy-done((bf16[512,2048]{1,0:T(8,128)(2,1)S(1)}, bf16[512,2048]{1,0:T(8,128)(2,1)}, u32[]{:S(2)}) %copy-start) | copy-done | bytes 2097176
  2.2 0.0 copy-start.1
  2.2 1.2 copy-done.1
  3.5 0.0 copy-start.2
  3.5 0.9 copy-done.2
  4.4 0.0 copy-start.3
  4.4 0.9 copy-done.3
  5.4 0.0 copy-start.4
  5.4 0.8 copy-done.4
  6.1 0.0 copy-start.5
  6.1 0.8 copy-done.5
  6.9 0.0 copy-start.6
  6.9 0.8 copy-done.6
  7.6 0.0 copy-start.7
  7.6 0.7 copy-done.7
  8.3 0.0 copy-start.8
  8.4 0.7 copy-done.8
  9.0 0.0 copy-start.9
  9.0 0.7 copy-done.9
  9.7 0.0 copy-start.10
  9.7 0.7 copy-done.10
  10.4 0.7 copy-done.11
  11.1 108.3 %training_step.1 = (bf16[256,512]{1,0:T(8,128)(2,1)S(1)}, bf16[256,512]{1,0:T(8,128)(2,1)S(1)}, f32[32,256]{1,0:T(8,128)S(1)}, f32[32,256]{1,0:T(8,128)S(1)}, f3...) custom-call(bf16[256,512]{1,0:T(8,128)(2,1)S(1)} %bitcast.27, ...), custom_call_target="tpu_custom_call" | custom-call | flops 4000000000 | bytes 6000000 | tf_op jit(solution)/shard_map/training_step/pallas_call | solution.py:375
  119.4 0.7 copy.28
  120.1 0.7 copy.29
  120.8 0.6 copy.30
  121.5 0.6 copy.31
  122.1 0.6 copy.32
  122.7 0.6 copy.33
  123.3 0.6 copy.34
  123.9 0.6 copy.35
  (1 shorter events, 0.0 us)
Async XLA Ops:
  0.6 1.6 %copy-start = (bf16[512,2048]{1,0:T(8,128)(2,1)S(1)}, bf16[512,2048]{1,0:T(8,128)(2,1)}, u32[]{:S(2)}) copy-start(bf16[512,2048]{1,0:T(8,128)(2,1)} %basis_hbm.1) | copy-start | bytes 6291460
  2.2 1.2 copy-start.1
  3.5 0.9 copy-start.2
  4.4 0.9 copy-start.3
  5.4 0.8 copy-start.4
  6.1 0.8 copy-start.5
  6.9 0.8 copy-start.6
  7.6 0.7 copy-start.7
  8.3 0.7 copy-start.8
  9.0 0.7 copy-start.9
  9.7 0.7 copy-start.10
  10.4 0.7 copy-start.11
